TPU v7x, 512 devices: a whole 4x4x16 slice. The times are simulated.
512 devices in a mesh: fsdp: 64 (over x, y, z_lo), node: 8 (over z_hi, core).
Axes of the slice: x: 4, y: 4, z: 16 (z_hi: 4, z_lo: 4; z = z_hi * 4 + z_lo), core: 2. Of those that a mesh axis runs over, the one named last changes fastest.
Arguments:
- tokens: bfloat16 [24576, 4096], P('fsdp'), may hold values from -16 to 16
- norm_gain: bfloat16 [4096], replicated, may hold values from 0.5 to 1.5
- kv_cotangent: bfloat16 [24576, 2048], P('fsdp', 'node'), may hold values from -6 to 6
- weight_codes: bfloat16 [8, 4096, 256], P('node', 'fsdp'), may hold values from -127 to 127, as said below
- block_scales: bfloat16 [8, 4096], P('node', 'fsdp'), may hold values from 6.9618225e-05 to 0.0006980896
Outputs:
- d_tokens: bfloat16 [24576, 4096], P(('fsdp', 'node'))
- gain_grad: float32 [4096], replicated
- weight_grads: float32 [8, 4096, 256], P('node', 'fsdp')
Inputs may be any that keep to these rules, and one draw needn't show every extreme that they name: weight_codes holds whole numbers.
All inputs are finite; a program needn't handle non-finite values.
Results may differ from a plain program's by a relative error of at most 0.018.
Values may be sent and summed in bfloat16 or wider, within the bound.
A program may use at most 64 MiB of HBM per device.

v0:
```python
import jax
import jax.numpy as jnp
from jax import lax
from jax.sharding import PartitionSpec as P


def local(tokens, norm_gain, kv_cotangent, weight_codes, block_scales):
    count_near = lax.axis_size("node")
    own_rows = weight_codes.shape[1]
    width_block = weight_codes.shape[2]
    width_kv = kv_cotangent.shape[1]
    all_codes, all_scales = (
        lax.all_gather(weight_codes, "fsdp", axis=1, tiled=True),
        lax.all_gather(block_scales, "fsdp", axis=1, tiled=True),
    )
    weights = (all_codes.astype(jnp.float32) * all_scales.astype(jnp.float32)[:, :, None]).astype(
        jnp.bfloat16
    )
    weights = weights.reshape(-1, width_kv)
    tok_float = tokens.astype(jnp.float32)
    inv_root = lax.rsqrt(jnp.mean(tok_float * tok_float, axis=-1, keepdims=True) + 1e-05)
    x_hat = tok_float * inv_root
    gain_float = norm_gain.astype(jnp.float32)
    x_norm = (x_hat * gain_float).astype(jnp.bfloat16)
    partial_value = jnp.dot(kv_cotangent, weights.T, preferred_element_type=jnp.float32).astype(
        jnp.bfloat16
    )
    share = tokens.shape[0] // count_near
    start_row = lax.axis_index("node") * share
    summed = lax.psum(partial_value, "node").astype(jnp.float32)
    d_norm = lax.dynamic_slice_in_dim(summed, start_row, share, 0)
    hat_rows = lax.dynamic_slice_in_dim(x_hat, start_row, share, 0)
    root_rows = lax.dynamic_slice_in_dim(inv_root, start_row, share, 0)
    gain_grad = lax.psum(jnp.sum(d_norm * hat_rows, axis=0), ("fsdp", "node"))
    scaled = gain_float * d_norm
    stat = jnp.mean(scaled * hat_rows, axis=-1, keepdims=True)
    d_tokens = (root_rows * (scaled - hat_rows * stat)).astype(jnp.bfloat16)
    product = lax.dot_general(
        x_norm, kv_cotangent, (((0,), (0,)), ((), ())), preferred_element_type=jnp.float32
    )
    grads = lax.psum_scatter(product, "fsdp", scatter_dimension=0, tiled=True)
    return (d_tokens, gain_grad, grads.reshape(1, own_rows, width_block))


def solution(mesh):
    placed = (P("fsdp", None), P(), P("fsdp", "node"), P("node", "fsdp", None), P("node", "fsdp"))
    return jax.shard_map(
        local,
        mesh=mesh,
        in_specs=placed,
        out_specs=(P(("fsdp", "node"), None), P(), P("node", "fsdp", None)),
        check_vma=False,
    )
```

profile of v0, /device:TPU:128, one launch (start us, length us, event | category | flops | bytes accessed | tf_op | source)
XLA Modules:
  0.0 942.8 jit_solution(18100922778100524641)
XLA Ops:
  7.2 0.0 copy-start
  7.2 0.0 all-gather.2.cloned.1.call-start
  7.2 0.7 all-gather.2.cloned.1.call-update
  7.9 0.0 all-reduce.3.cloned.1.call-start
  8.0 1.3 dynamic-slice.4
  9.9 0.9 dynamic-update-slice
  10.8 195.4 %all-reduce = bf16[4096]{0:T(1024)(128)(2,1)S(1)} all-reduce(bf16[4096]{0:T(1024)(128)(2,1)S(1)} %dynamic-update-slice), channel_id=1, replica_groups=mesh['fsdp'=64,'node'=8] {'fsdp'}, use_global_device_ids=true, to_apply=%add | all-reduce | flops 4096 | bytes 16384
  206.2 162.7 %all-gather.2.cloned.1.call-done = bf16[1,4096,256]{2,1,0:T(8,128)(2,1)} async-done(((bf16[1,64,256]{2,1,0:T(8,128)(2,1)}), bf16[1,4096,256]{2,1,0:T(8,128)(2,1)}) %all-gather.2.cloned.1.call-update) | async-done | bytes 2097168 | tf_op jit(solution)/shard_map/all_gather | solution.py:13
  368.8 0.0 copy-done
  368.8 4.6 fusion.1
  373.5 0.0 copy-start.1
  373.5 0.0 all-reduce.3.cloned.1.call-update
  373.5 0.0 reduce-scatter.2.cloned.1.call-start
  373.6 0.6 copy-done.1
  374.2 3.4 copy.8
  377.6 0.8 fusion
  378.4 2.9 fusion.2
  381.3 0.0 reduce-scatter.2.cloned.1.call-update
  381.3 0.1 dynamic-slice.3
  381.4 3.1 convert_multiply_fusion
  384.5 155.6 %all-reduce.3.cloned.1.call-done = bf16[384,4096]{0,1:T(8,128)(2,1)} async-done(((bf16[384,4096]{0,1:T(8,128)(2,1)}), bf16[384,4096]{0,1:T(8,128)(2,1)}) %all-reduce.3.cloned.1.call-update) | async-done | bytes 3145744 | tf_op jit(solution)/shard_map/psum | solution.py:30
  540.1 4.0 fusion.9
  544.1 3.6 fusion.8
  547.7 1.1 copy.9
  548.8 109.0 %psum.15 = f32[4096]{0:T(1024)} all-reduce(f32[4096]{0:T(1024)S(1)} %get-tuple-element.6), channel_id=1, replica_groups=mesh['fsdp'=64,'node'=8] {'fsdp','node'}, use_global_device_ids=true, to_apply=%region_4.0 | all-reduce | flops 4096 | bytes 32768 | tf_op jit(solution)/shard_map/psum | solution.py:34
  657.8 278.5 %reduce-scatter.2.cloned.1.call-done = f32[64,256]{1,0:T(8,128)} async-done(((f32[4096,256]{1,0:T(8,128)}), f32[64,256]{1,0:T(8,128)}) %reduce-scatter.2.cloned.1.call-update) | async-done | bytes 65552 | tf_op jit(solution)/shard_map/reduce_scatter | solution.py:41
  (5 shorter events, 0.0 us)
Async XLA Ops:
  7.2 361.7 %copy-start = (bf16[384,256]{1,0:T(8,128)(2,1)S(1)}, bf16[384,256]{1,0:T(8,128)(2,1)}, u32[]{:S(2)}) copy-start(bf16[384,256]{1,0:T(8,128)(2,1)} %param.7) | copy-start | bytes 589828
  7.2 361.7 %all-gather.2.cloned.1.call-start = ((), (), s32[]{:S(2)}) async-start(), calls=%async_computation.1 | async-start | bytes 2129920 | tf_op jit(solution)/shard_map/all_gather | solution.py:13
  7.9 532.2 %all-reduce.3.cloned.1.call-start = ((), (), s32[]{:S(2)}) async-start(), calls=%async_computation.2 | async-start | bytes 6291456 | tf_op jit(solution)/shard_map/psum | solution.py:30
  373.5 0.7 copy-start.1
  373.5 562.7 %reduce-scatter.2.cloned.1.call-start = ((), (), s32[]{:S(2)}) async-start(), calls=%async_computation.3 | async-start | bytes 4259840 | tf_op jit(solution)/shard_map/reduce_scatter | solution.py:41
Sparse Core Ops, SparseCore 0:
  10.1 358.6 all-gather.1
  373.6 166.4 all-reduce.2
  543.5 392.7 reduce-scatter.1
where the time goes:
time: 943 us
  waiting for transfers between devices  597 us (63%)
  blocking collectives  304 us (32%)
  between operations  14.5 us (2%)
  other arithmetic  11.4 us (1%)
    reduce_scatter x1, waiting for transfers between devices, local(): grads = lax.psum_scatter(product, 'fsdp', scatter_dimension=0, tiled=True)  278 us
    unnamed x1, blocking collectives  195 us
    all_gather x1, waiting for transfers between devices, local(): lax.all_gather(weight_codes, 'fsdp', axis=1, tiled=True)  163 us
    psum x1, waiting for transfers between devices, local(): summed = lax.psum(partial_value, 'node').astype(jnp.float32)  156 us
    psum x1, blocking collectives, local(): gain_grad = lax.psum(jnp.sum(d_norm * hat_rows, axis=0), ('fsdp', 'node'))  109 us
  transfers between devices with their start and end apart: 3, of which 3 were waited for; matrix products, arithmetic and copies ran while one was open for 2% of the time, Pallas kernels for 0%

commit v1 on v0

v1 whole, which is shorter than its diff:
```python
import jax
import jax.numpy as jnp
from jax import lax
from jax.experimental import pallas as pl
from jax.experimental.pallas import tpu as pltpu
from jax.sharding import PartitionSpec as P

MESH = pl.DeviceIdType.MESH
F32 = jnp.float32
BF16 = jnp.bfloat16
ORDER = (2, 1, 3, 0)


def kernel(
    tok_hbm, gain_ref, kv_hbm, codes_ref, scales_ref,
    dt_ref, gg_ref, wg_ref,
    cot, wbuf, tok_v, xhat, root, xs, xall, xn, xt,
    dn, dsend, drecv, dout, din,
    gs, gr, s_own, ss, sr,
    g_own, g_sib, g_z, g_xy,
    tok_sem, own_sem, za_s, za_r, w_s, w_r, x_s, x_r, xb_s, xb_r,
    c_s, c_r, g_s, g_r, q_s, q_r, e_s, e_r, a_s, a_r,
    gb_s, gb_r, gz_s, gz_r, gx_s, gx_r,
):
    fs, nd = lax.axis_index("fsdp"), lax.axis_index("node")
    zl, p = lax.rem(fs, 4), lax.div(fs, 4)
    x, y = lax.div(p, 4), lax.rem(p, 4)
    zh, c = lax.div(nd, 2), lax.rem(nd, 2)
    z = zh * 4 + zl

    def plane(xx, yy):
        return ((xx * 4 + yy) * 4 + zl, nd)

    def column(zz):
        return (p * 4 + lax.rem(zz, 4), lax.div(zz, 4) * 2 + c)

    sibling = (fs, zh * 2 + (1 - c))

    def send(src, dst, send_sem, recv_sem, device):
        pltpu.make_async_remote_copy(
            src_ref=src, dst_ref=dst, send_sem=send_sem, recv_sem=recv_sem,
            device_id=device, device_id_type=MESH,
        ).start()

    def wait(ref, sem):
        pltpu.make_async_copy(ref, ref, sem).wait()

    tok_copy = pltpu.make_async_copy(
        tok_hbm.at[pl.ds(pl.multiple_of(nd * 48, 16), 48)], tok_v, tok_sem
    )
    tok_copy.start()
    own_copy = pltpu.make_async_copy(
        kv_hbm.at[pl.ds(pl.multiple_of(zh * 96, 16), 96)], cot.at[0, x, y], own_sem
    )
    own_copy.start()

    barrier = pltpu.get_barrier_semaphore()

    def greet(o, carry):
        there = plane(lax.rem(x + lax.div(o, 4), 4), lax.rem(y + lax.rem(o, 4), 4))
        pl.semaphore_signal(barrier, inc=1, device_id=there, device_id_type=MESH)
        there = column(lax.rem(z + o, 16))
        pl.semaphore_signal(barrier, inc=1, device_id=there, device_id_type=MESH)
        return carry

    lax.fori_loop(1, 16, greet, 0)
    pl.semaphore_signal(barrier, inc=1, device_id=sibling, device_id_type=MESH)

    rows = lax.broadcasted_iota(jnp.int32, (64, 64), 0)
    cols = lax.broadcasted_iota(jnp.int32, (64, 64), 1)
    scales = jnp.broadcast_to(scales_ref[...].astype(F32), (64, 64))
    diagonal = jnp.where(rows == cols, scales, 0.0).astype(BF16)
    wbuf[z] = jnp.dot(diagonal, codes_ref[0], preferred_element_type=F32).astype(BF16)

    pl.semaphore_wait(barrier, 31)

    def share(t):
        there = lax.rem(zh + t, 4)
        slot = (4 - t) % 4
        send(
            kv_hbm.at[pl.ds(pl.multiple_of(there * 96, 16), 96)], cot.at[slot, x, y],
            za_s.at[t - 1], za_r.at[slot - 1], (fs, there * 2 + c),
        )

    def w_slot(o):
        return wbuf.at[lax.rem(z + o + 16, 16)]

    def w_send(s):
        send(w_slot(-s), w_slot(-s), w_s.at[s], w_r.at[s], column(lax.rem(z + 1, 16)))
        if s < 7:
            send(w_slot(s), w_slot(s), w_s.at[8 + s], w_r.at[8 + s], column(lax.rem(z + 15, 16)))

    def w_wait(s):
        wait(w_slot(-1 - s), w_r.at[s])
        if s < 7:
            wait(w_slot(1 + s), w_r.at[8 + s])

    share(2)
    w_send(0)
    share(1)
    share(3)

    tok_copy.wait()
    for b in range(3):
        part = pl.ds(16 * b, 16)
        t = tok_v[part].astype(F32)
        inv = lax.rsqrt(jnp.mean(t * t, axis=-1, keepdims=True) + 1e-05)
        hat = t * inv
        xhat[part] = hat
        root[part] = jnp.broadcast_to(inv, (16, 128))
        for q in range(16):
            xs[q, part] = hat[:, 256 * q : 256 * (q + 1)].astype(BF16)

    def x_push(o, carry):
        xx, yy = lax.rem(x + lax.div(o, 4), 4), lax.rem(y + lax.rem(o, 4), 4)
        send(xs.at[xx * 4 + yy], xall.at[p, c], x_s, x_r, plane(xx, yy))
        return carry

    lax.fori_loop(1, 16, x_push, 0)
    xall[p, c] = xs[p]

    def at(first, o1, o2):
        if first == 0:
            return lax.rem(x + o1 + 4, 4), lax.rem(y + o2 + 4, 4)
        return lax.rem(x + o2 + 4, 4), lax.rem(y + o1 + 4, 4)

    def one(rel, r, o):
        xx, yy = at(r, o, 0)
        return cot.at[rel, xx, yy, pl.ds(48 * r, 48)]

    def line(rel, r, o):
        xx, yy = at(r, 0, o)
        if r == 0:
            return cot.at[rel, pl.ds(0, 4), yy, pl.ds(0, 48)]
        return cot.at[rel, xx, pl.ds(0, 4), pl.ds(48, 48)]

    def push(ref, rel, r, k, o1, o2):
        send(ref, ref, c_s.at[rel, r, k], c_r.at[rel, r, k], plane(*at(r, o1, o2)))

    def stage(i, st):
        rel = ORDER[i]
        if st == 0:
            if rel:
                wait(cot.at[rel, x, y], za_r.at[rel - 1])
            else:
                own_copy.wait()
        for r in range(2):
            d = 1 if (i + r) % 2 == 0 else -1
            kd, ko = (0, 1) if d == 1 else (1, 0)
            got = lambda ref, k: wait(ref, c_r.at[rel, r, k])
            if st == 0:
                push(one(rel, r, 0), rel, r, 0, 1, 0)
                push(one(rel, r, 0), rel, r, 1, -1, 0)
            elif st == 1:
                got(one(rel, r, -d), kd)
                push(one(rel, r, -d), rel, r, 2, d, 0)
            elif st == 2:
                got(one(rel, r, d), ko)
                got(one(rel, r, 2), 2)
                push(line(rel, r, 0), rel, r, 3, 0, 1)
                push(line(rel, r, 0), rel, r, 4, 0, -1)
            elif st == 3:
                got(line(rel, r, -d), 3 + kd)
                push(line(rel, r, -d), rel, r, 5, 0, d)
            else:
                got(line(rel, r, d), 3 + ko)
                got(line(rel, r, 2), 5)

    def grads(rel):
        block = cot[rel].reshape(1536, 256)
        gs[rel] = jnp.dot(xt[...], block, preferred_element_type=F32).astype(BF16).reshape(4, 64, 256)
        for t in range(1, 4):
            there = lax.rem(zl + t, 4)
            send(gs.at[rel, there], gr.at[rel, t - 1], g_s.at[rel], g_r.at[rel], (p * 4 + there, nd))

    def near_sum(rel):
        wait(gr.at[rel], g_r.at[rel])
        total = gs[rel, zl].astype(F32)
        for t in range(3):
            total = total + gr[rel, t].astype(F32)
        if rel:
            ss[rel - 1] = total.astype(BF16)
            there = lax.rem(zh + rel, 4)
            send(ss.at[rel - 1], sr.at[rel - 1], q_s.at[rel - 1], q_r.at[rel - 1], (fs, there * 2 + c))
        else:
            s_own[...] = total

    def times_w(rel, xi):
        head = wbuf[pl.ds(lax.rem(zh + rel, 4) * 4, 4)].reshape(256, 256)
        block = cot[rel, xi].reshape(384, 256)
        return lax.dot_general(block, head, (((1,), (1,)), ((), ())), preferred_element_type=F32)

    gain_here = gain_ref[:, pl.ds(pl.multiple_of(p * 256, 256), 256)].astype(F32)

    for t in range(8):
        if t < 7:
            w_wait(t)
            w_send(t + 1)
        if t == 7:
            w_wait(7)
        for i in range(4):
            if 0 <= t - i < 5 and not (t == 7 and i == 3):
                stage(i, t - i)
        if t == 1:
            wait(xall.at[pl.ds(0, 15), 0], x_r)
            send(xall.at[pl.ds(0, 16), c], xall.at[pl.ds(0, 16), c], xb_s, xb_r, sibling)
        if t == 2:
            wait(xall.at[pl.ds(0, 16), 1 - c], xb_r)
            for q in range(16):
                xn[pl.ds(96 * q, 96)] = (xall[q].reshape(96, 256).astype(F32) * gain_here).astype(BF16)
        if t == 3:
            for q in range(12):
                xt[:, 128 * q : 128 * (q + 1)] = xn[128 * q : 128 * (q + 1)].T
        if 4 <= t < 7:
            grads(ORDER[t - 4])
        if t >= 6:
            near_sum(ORDER[t - 6])

    def three(xi, carry):
        total = times_w(2, xi) + times_w(1, xi) + times_w(3, xi)
        dn[pl.ds(4 * xi, 4)] = total.reshape(4, 2, 48, 256)
        return carry

    lax.fori_loop(0, 4, three, 0)
    stage(3, 4)

    def last(j, gain_sum):
        xi = lax.rem(x + j, 4)
        mine = pl.ds(4 * xi, 4)
        total = dn[mine] + times_w(0, xi).reshape(4, 2, 48, 256)
        dn[mine] = total
        dsend[mine] = dn[mine, 1 - c].astype(BF16)
        send(dsend.at[mine], drecv.at[mine], e_s.at[j], e_r.at[j], sibling)
        products = (total * xall[mine].astype(F32)).reshape(384, 256)
        return gain_sum + jnp.sum(products, axis=0, keepdims=True)

    g_own[...] = lax.fori_loop(0, 4, last, jnp.zeros((1, 256), F32))
    send(g_own, g_sib, gb_s, gb_r, sibling)
    grads(0)

    def turn(j, carry):
        xi = lax.rem(x + j, 4)
        mine = pl.ds(4 * xi, 4)
        wait(drecv.at[mine], e_r.at[j])
        dout[mine] = (dn[mine, c] + drecv[mine].astype(F32)).astype(BF16)

        def spread(o, inner):
            yy = lax.rem(y + o, 4)

            @pl.when(j * 4 + o > 0)
            def _():
                send(dout.at[xi * 4 + yy], din.at[p], a_s, a_r, plane(xi, yy))

            return inner

        return lax.fori_loop(0, 4, spread, carry)

    lax.fori_loop(0, 4, turn, 0)
    din[p] = dout[p]

    wait(g_sib, gb_r)
    g_z[z] = g_own[...] + g_sib[...]

    def g_push(o, carry):
        send(g_z.at[z], g_z.at[z], gz_s, gz_r, column(lax.rem(z + o, 16)))
        return carry

    lax.fori_loop(1, 16, g_push, 0)
    near_sum(3)
    near_sum(0)

    wait(g_z.at[pl.ds(0, 15)], gz_r)
    g_xy[p] = jnp.sum(g_z[...], axis=0)

    def g_spread(o, carry):
        xx, yy = lax.rem(x + lax.div(o, 4), 4), lax.rem(y + lax.rem(o, 4), 4)
        send(g_xy.at[p], g_xy.at[p], gx_s, gx_r, plane(xx, yy))
        return carry

    lax.fori_loop(1, 16, g_spread, 0)

    wait(din.at[pl.ds(0, 15)], a_r)
    gain_all = gain_ref[...].astype(F32)
    for b in range(3):
        part = pl.ds(16 * b, 16)
        d = jnp.concatenate([din[q, part] for q in range(16)], axis=1).astype(F32)
        scaled = gain_all * d
        hat = xhat[part]
        stat = jnp.mean(scaled * hat, axis=-1, keepdims=True)
        dt_ref[part] = (root[part, 0:1] * (scaled - hat * stat)).astype(BF16)

    total = s_own[...]
    for k in range(3):
        wait(sr.at[k], q_r.at[k])
        total = total + sr[k].astype(F32)
    wg_ref[...] = total

    wait(g_xy.at[pl.ds(0, 15)], gx_r)
    gg_ref[...] = g_xy[...]

    for t in range(3):
        wait(cot.at[0, 0, 0], za_s.at[t])
        wait(ss.at[t], q_s.at[t])
    for s in range(15):
        wait(wbuf.at[0], w_s.at[s])
    wait(xs.at[pl.ds(0, 15)], x_s)
    wait(xall.at[pl.ds(0, 16), 0], xb_s)
    for rel in range(4):
        for r in range(2):
            for k in range(6):
                wait(one(rel, r, 0) if k < 3 else line(rel, r, 0), c_s.at[rel, r, k])
        wait(gr.at[rel], g_s.at[rel])
        wait(dsend.at[pl.ds(0, 4)], e_s.at[rel])
    wait(dout.at[pl.ds(0, 15)], a_s)
    wait(g_own, gb_s)
    wait(g_z.at[pl.ds(0, 15)], gz_s)
    wait(g_xy.at[pl.ds(0, 15)], gx_s)


def local(tokens, norm_gain, kv_cotangent, weight_codes, block_scales):
    vmem, dma = pltpu.VMEM, pltpu.SemaphoreType.DMA
    any_spec, vmem_spec = pl.BlockSpec(memory_space=pl.ANY), pl.BlockSpec(memory_space=pltpu.VMEM)
    d_tokens, gain_grad, grads = pl.pallas_call(
        kernel,
        out_shape=(
            jax.ShapeDtypeStruct((48, 4096), BF16),
            jax.ShapeDtypeStruct((16, 1, 256), F32),
            jax.ShapeDtypeStruct((64, 256), F32),
        ),
        in_specs=[any_spec, vmem_spec, any_spec, vmem_spec, vmem_spec],
        out_specs=[vmem_spec] * 3,
        scratch_shapes=[
            vmem((4, 4, 4, 96, 256), BF16),
            vmem((16, 64, 256), BF16),
            vmem((48, 4096), BF16),
            vmem((48, 4096), F32),
            vmem((48, 128), F32),
            vmem((16, 48, 256), BF16),
            vmem((16, 2, 48, 256), BF16),
            vmem((1536, 256), BF16),
            vmem((256, 1536), BF16),
            vmem((16, 2, 48, 256), F32),
            vmem((16, 48, 256), BF16),
            vmem((16, 48, 256), BF16),
            vmem((16, 48, 256), BF16),
            vmem((16, 48, 256), BF16),
            vmem((4, 4, 64, 256), BF16),
            vmem((4, 3, 64, 256), BF16),
            vmem((64, 256), F32),
            vmem((3, 64, 256), BF16),
            vmem((3, 64, 256), BF16),
            vmem((1, 256), F32),
            vmem((1, 256), F32),
            vmem((16, 1, 256), F32),
            vmem((16, 1, 256), F32),
            dma, dma,
            dma((3,)), dma((3,)),
            dma((15,)), dma((15,)),
            dma, dma, dma, dma,
            dma((4, 2, 6)), dma((4, 2, 6)),
            dma((4,)), dma((4,)),
            dma((3,)), dma((3,)),
            dma((4,)), dma((4,)),
            dma, dma, dma, dma, dma, dma, dma, dma,
        ],
        compiler_params=pltpu.CompilerParams(
            collective_id=0, has_side_effects=True, vmem_limit_bytes=40 * 1024 * 1024
        ),
    )(tokens, norm_gain.reshape(1, 4096), kv_cotangent, weight_codes, block_scales)
    return d_tokens, gain_grad.reshape(4096), grads.reshape(1, 64, 256)


def solution(mesh):
    placed = (P("fsdp", None), P(), P("fsdp", "node"), P("node", "fsdp", None), P("node", "fsdp"))
    return jax.shard_map(
        local,
        mesh=mesh,
        in_specs=placed,
        out_specs=(P(("fsdp", "node"), None), P(), P("node", "fsdp", None)),
        check_vma=False,
    )
```

time: 943 us -> 84.2 us (0.09)
  the two profiles are of different devices: /device:TPU:128 before, /device:TPU:1 now
where the time goes in v1:
time: 84.2 us; the launch traced here: 83.7 us
  Pallas kernels  76.1 us (90%)
  local copies, waits for them, and re-layouts  6.92 us (8%)
    pallas_call x1, Pallas kernels, local(): pl.pallas_call(kernel, out_shape=(jax.ShapeDtypeStruct((48, 4096), BF16),...  76.1 us
    unnamed x11, local copies, waits for them, and re-layouts  6.21 us

profile of v1, /device:TPU:1, one launch (start us, length us, event | category | flops | bytes accessed | tf_op | source)
XLA Modules:
  0.0 83.7 jit_solution(17577838215543370736)
XLA Ops:
  0.6 0.7 reshape.15.gain_ref
  1.3 0.0 copy-start
  1.4 1.9 %copy-done = bf16[384,4096]{1,0:T(8,128)(2,1)S(1)} copy-done((bf16[384,4096]{1,0:T(8,128)(2,1)S(1)}, bf16[384,4096]{1,0:T(8,128)(2,1)}, u32[]{:S(2)}) %copy-start) | copy-done | bytes 3145752
  3.2 0.0 copy-start.1
  3.2 0.9 %copy-done.1 = bf16[384,256]{1,0:T(8,128)(2,1)S(1)} copy-done((bf16[384,256]{1,0:T(8,128)(2,1)S(1)}, bf16[384,256]{1,0:T(8,128)(2,1)}, u32[]{:S(2)}) %copy-start.1) | copy-done | bytes 196632
  4.2 0.0 copy-start.2
  4.2 0.8 copy-done.2
  4.9 0.0 copy-start.3
  4.9 0.7 copy-done.3
  5.6 76.1 %shard_map.76 = (bf16[48,4096]{1,0:T(8,128)(2,1)S(1)}, f32[16,1,256]{2,1,0:T(1,128)S(1)}, f32[64,256]{1,0:T(8,128)S(1)}) custom-call(bf16[384,4096]{1,0:T(8,128)(2,1)S(1)} %copy-done, bf16[1,4096]{1,0:T(2,128)(2,1)S(1)} %reshape.15.gain_ref, bf16[384,256]{1,0:T(8,128)(2,1)S(1)} %copy-done.1, bf16[1,64,256]{2,1,0:T(8,128)(2,1)S(1)} %copy-done.2, ...), custom_call_target="tpu_custom_call" | custom-call | tf_op jit(solution)/shard_map/pallas_call | solution.py:323
  81.7 0.7 copy.11
  82.4 0.6 copy.12
  83.0 0.6 copy.13
Async XLA Ops:
  1.3 1.9 %copy-start = (bf16[384,4096]{1,0:T(8,128)(2,1)S(1)}, bf16[384,4096]{1,0:T(8,128)(2,1)}, u32[]{:S(2)}) copy-start(bf16[384,4096]{1,0:T(8,128)(2,1)} %tok_hbm.1) | copy-start | bytes 9437188
  3.2 0.9 %copy-start.1 = (bf16[384,256]{1,0:T(8,128)(2,1)S(1)}, bf16[384,256]{1,0:T(8,128)(2,1)}, u32[]{:S(2)}) copy-start(bf16[384,256]{1,0:T(8,128)(2,1)} %kv_hbm.1) | copy-start | bytes 589828
  4.2 0.8 copy-start.2
  4.9 0.7 copy-start.3

commit v2 on v1

v2 whole, which is shorter than its diff:
```python
import jax
import jax.numpy as jnp
from jax import lax
from jax.experimental import pallas as pl
from jax.experimental.pallas import tpu as pltpu
from jax.sharding import PartitionSpec as P

MESH = pl.DeviceIdType.MESH
F32 = jnp.float32
BF16 = jnp.bfloat16
W_GOT = ((), (-1, -2, 1, 2), (-3, -4, 3, 4), (-5, -6, 5, 6), (-7, -8, 7))
ORDER = (0, 1, 3, 2)


def kernel(
    tok_hbm, gain_ref, kv_hbm, codes_hbm, scales_hbm,
    dt_ref, gg_ref, wg_ref,
    codes_ref, scales_ref, cot, wbuf, tok_v, xhat, root, xs, xall, xn, xt,
    dn, dsend, drecv, dout, din,
    gs, gr, s_own, ss, sr,
    g_z, g_xy,
    code_sem, scale_sem, tok_sem, own_sem, za_s, za_r, w_s, w_r, x_s, x_r, xb_s, xb_r,
    c_s, c_r, g_s, g_r, q_s, q_r, e_s, e_r, a_s, a_r,
    gz_s, gz_r, gx_s, gx_r,
):
    fs, nd = lax.axis_index("fsdp"), lax.axis_index("node")
    zl, p = lax.rem(fs, 4), lax.div(fs, 4)
    x, y = lax.div(p, 4), lax.rem(p, 4)
    zh, c = lax.div(nd, 2), lax.rem(nd, 2)
    z = zh * 4 + zl

    def plane(xx, yy):
        return ((xx * 4 + yy) * 4 + zl, nd)

    def column(zz, core=c):
        return (p * 4 + lax.rem(zz, 4), lax.div(zz, 4) * 2 + core)

    sibling = (fs, zh * 2 + (1 - c))

    def send(src, dst, send_sem, recv_sem, device):
        pltpu.make_async_remote_copy(
            src_ref=src, dst_ref=dst, send_sem=send_sem, recv_sem=recv_sem,
            device_id=device, device_id_type=MESH,
        ).start()

    def wait(ref, sem):
        pltpu.make_async_copy(ref, ref, sem).wait()

    tok_copy = pltpu.make_async_copy(
        tok_hbm.at[pl.ds(pl.multiple_of(nd * 48, 16), 48)], tok_v, tok_sem
    )
    code_copy = pltpu.make_async_copy(codes_hbm, codes_ref, code_sem)
    scale_copy = pltpu.make_async_copy(scales_hbm, scales_ref, scale_sem)
    code_copy.start()
    scale_copy.start()
    tok_copy.start()
    own_copy = pltpu.make_async_copy(
        kv_hbm.at[pl.ds(pl.multiple_of(zh * 96, 16), 96)], cot.at[0, x, y], own_sem
    )
    own_copy.start()

    barrier = pltpu.get_barrier_semaphore()

    def column_any(o):
        return column(lax.rem(z + lax.div(o, 2), 16), lax.rem(c + o, 2))

    def greet_column(o, carry):
        pl.semaphore_signal(barrier, inc=1, device_id=column_any(lax.rem(o + 15, 32)), device_id_type=MESH)
        return carry

    def greet_plane(o, carry):
        there = plane(lax.rem(x + lax.div(o, 4), 4), lax.rem(y + lax.rem(o, 4), 4))
        pl.semaphore_signal(barrier, inc=1, device_id=there, device_id_type=MESH)
        return carry

    lax.fori_loop(0, 17, greet_column, 0)
    lax.fori_loop(18, 32, greet_column, 0)
    lax.fori_loop(1, 16, greet_plane, 0)

    code_copy.wait()
    scale_copy.wait()
    rows = lax.broadcasted_iota(jnp.int32, (64, 64), 0)
    cols = lax.broadcasted_iota(jnp.int32, (64, 64), 1)
    scales = jnp.broadcast_to(scales_ref[...].astype(F32), (64, 64))
    diagonal = jnp.where(rows == cols, scales, 0.0).astype(BF16)
    wbuf[z] = jnp.dot(diagonal, codes_ref[0], preferred_element_type=F32).astype(BF16)

    tok_copy.wait()
    for b in range(3):
        part = pl.ds(16 * b, 16)
        t = tok_v[part].astype(F32)
        inv = lax.rsqrt(jnp.mean(t * t, axis=-1, keepdims=True) + 1e-05)
        hat = t * inv
        xhat[part] = hat
        root[part] = jnp.broadcast_to(inv, (16, 128))
        for q in range(16):
            xs[q, part] = hat[:, 256 * q : 256 * (q + 1)].astype(BF16)
    xall[p, c] = xs[p]

    pl.semaphore_wait(barrier, 46)

    def share(t):
        there = lax.rem(zh + t, 4)
        slot = (4 - t) % 4
        for r in range(2):
            send(
                kv_hbm.at[pl.ds(pl.multiple_of(there * 96 + 48 * r, 16), 48)],
                cot.at[slot, x, y, pl.ds(48 * r, 48)],
                za_s.at[t - 1, r], za_r.at[slot - 1, r], (fs, there * 2 + c),
            )

    def w_slot(o):
        return wbuf.at[lax.rem(z + o + 16, 16)]

    def w_index(o):
        return -o - 1 if o < 0 else 7 + o

    def w_push(o, t):
        k = w_index(o - t)
        send(w_slot(o), w_slot(o), w_s.at[k], w_r.at[k], column(lax.rem(z + t + 16, 16)))

    def w_round(n):
        for o in W_GOT[n]:
            wait(w_slot(o), w_r.at[w_index(o)])
        if n == 0:
            for t in (1, -1, 2, -2):
                w_push(0, t)
        elif n < 4:
            for o in W_GOT[n]:
                if o != 6:
                    w_push(o, 2 if o < 0 else -2)

    def x_push(o, carry):
        xx, yy = lax.rem(x + lax.div(o, 4), 4), lax.rem(y + lax.rem(o, 4), 4)
        send(xs.at[xx * 4 + yy], xall.at[p, c], x_s, x_r, plane(xx, yy))
        return carry

    def at(first, o1, o2):
        if first == 0:
            return lax.rem(x + o1 + 4, 4), lax.rem(y + o2 + 4, 4)
        return lax.rem(x + o2 + 4, 4), lax.rem(y + o1 + 4, 4)

    def one(rel, r, o):
        xx, yy = at(r, o, 0)
        return cot.at[rel, xx, yy, pl.ds(48 * r, 48)]

    def line(rel, r, o):
        xx, yy = at(r, 0, o)
        if r == 0:
            return cot.at[rel, pl.ds(0, 4), yy, pl.ds(0, 48)]
        return cot.at[rel, xx, pl.ds(0, 4), pl.ds(48, 48)]

    def push(ref, rel, r, k, o1, o2):
        send(ref, ref, c_s.at[rel, r, k], c_r.at[rel, r, k], plane(*at(r, o1, o2)))

    def stage(i, st):
        rel, direct = ORDER[i], i == 3
        if st == 0 and not rel:
            own_copy.wait()
        for r in range(2):
            d = 1 if (i + r) % 2 == 0 else -1
            kd, ko = (3, 4) if d == 1 else (4, 3)
            got = lambda ref, k: wait(ref, c_r.at[rel, r, k])
            if st == 0:
                if rel:
                    wait(one(rel, r, 0), za_r.at[rel - 1, r])
                push(one(rel, r, 0), rel, r, 2, 2, 0)
                push(one(rel, r, 0), rel, r, 0, 1, 0)
                push(one(rel, r, 0), rel, r, 1, -1, 0)
            elif st == 1:
                got(one(rel, r, -1), 0)
                got(one(rel, r, 1), 1)
                got(one(rel, r, 2), 2)
                if direct:
                    push(line(rel, r, 0), rel, r, 5, 0, 2)
                push(line(rel, r, 0), rel, r, 3, 0, 1)
                push(line(rel, r, 0), rel, r, 4, 0, -1)
            elif st == 2:
                got(line(rel, r, -d), kd)
                if not direct:
                    push(line(rel, r, -d), rel, r, 5, 0, d)
            else:
                got(line(rel, r, d), ko)
                got(line(rel, r, 2), 5)

    def grads(rel):
        block = cot[rel].reshape(1536, 256)
        gs[rel] = jnp.dot(xt[...], block, preferred_element_type=F32).astype(BF16).reshape(4, 64, 256)
        for t in range(1, 4):
            there = lax.rem(zl + t, 4)
            send(gs.at[rel, there], gr.at[rel, t - 1], g_s.at[rel], g_r.at[rel], (p * 4 + there, nd))

    def near_sum(rel):
        wait(gr.at[rel], g_r.at[rel])
        total = gs[rel, zl].astype(F32)
        for t in range(3):
            total = total + gr[rel, t].astype(F32)
        if rel:
            ss[rel - 1] = total.astype(BF16)
            there = lax.rem(zh + rel, 4)
            send(ss.at[rel - 1], sr.at[rel - 1], q_s.at[rel - 1], q_r.at[rel - 1], (fs, there * 2 + c))
        else:
            s_own[...] = total

    def times_w(rel, xi):
        head = wbuf[pl.ds(lax.rem(zh + rel, 4) * 4, 4)].reshape(256, 256)
        block = cot[rel, xi].reshape(384, 256)
        return lax.dot_general(block, head, (((1,), (1,)), ((), ())), preferred_element_type=F32)

    gain_here = gain_ref[:, pl.ds(pl.multiple_of(p * 256, 256), 256)].astype(F32)

    share(1)
    share(3)
    stage(0, 0)
    lax.fori_loop(1, 16, x_push, 0)
    stage(0, 1)
    w_round(0)
    share(2)
    stage(1, 0)
    stage(2, 0)
    stage(0, 2)
    wait(xall.at[pl.ds(0, 15), 0], x_r)
    send(xall.at[pl.ds(0, 16), c], xall.at[pl.ds(0, 16), c], xb_s, xb_r, sibling)
    w_round(1)
    stage(1, 1)
    stage(2, 1)
    stage(3, 0)
    stage(0, 3)
    wait(xall.at[pl.ds(0, 16), 1 - c], xb_r)
    for q in range(16):
        xn[pl.ds(96 * q, 96)] = (xall[q].reshape(96, 256).astype(F32) * gain_here).astype(BF16)
    for q in range(12):
        xt[:, 128 * q : 128 * (q + 1)] = xn[128 * q : 128 * (q + 1)].T
    w_round(2)
    stage(1, 2)
    stage(2, 2)
    grads(ORDER[0])
    stage(3, 1)
    w_round(3)
    stage(1, 3)
    grads(ORDER[1])
    stage(2, 3)
    grads(ORDER[2])
    near_sum(ORDER[0])
    w_round(4)

    def three(xi, carry):
        total = times_w(ORDER[0], xi) + times_w(ORDER[1], xi) + times_w(ORDER[2], xi)
        dn[pl.ds(4 * xi, 4)] = total.reshape(4, 2, 48, 256)
        return carry

    lax.fori_loop(0, 4, three, 0)
    near_sum(ORDER[1])
    near_sum(ORDER[2])
    stage(3, 2)
    stage(3, 3)

    def last(j, gain_sum):
        xi = lax.rem(x + j, 4)
        mine = pl.ds(4 * xi, 4)
        total = dn[mine] + times_w(ORDER[3], xi).reshape(4, 2, 48, 256)
        dn[mine] = total
        dsend[mine] = dn[mine, 1 - c].astype(BF16)
        send(dsend.at[mine], drecv.at[mine], e_s.at[j], e_r.at[j], sibling)
        products = (total * xall[mine].astype(F32)).reshape(384, 256)
        return gain_sum + jnp.sum(products, axis=0, keepdims=True)

    g_z[z * 2 + c] = lax.fori_loop(0, 4, last, jnp.zeros((1, 256), F32))

    def g_push(o, carry):
        send(g_z.at[z * 2 + c], g_z.at[z * 2 + c], gz_s, gz_r, column_any(lax.rem(o + 15, 32)))
        return carry

    lax.fori_loop(0, 17, g_push, 0)
    lax.fori_loop(18, 32, g_push, 0)
    grads(ORDER[3])

    def turn(j, carry):
        xi = lax.rem(x + j, 4)
        mine = pl.ds(4 * xi, 4)
        wait(drecv.at[mine], e_r.at[j])
        dout[mine] = (dn[mine, c] + drecv[mine].astype(F32)).astype(BF16)

        def spread(o, inner):
            yy = lax.rem(y + o, 4)

            @pl.when(j * 4 + o > 0)
            def _():
                send(dout.at[xi * 4 + yy], din.at[p], a_s, a_r, plane(xi, yy))

            return inner

        return lax.fori_loop(0, 4, spread, carry)

    lax.fori_loop(0, 4, turn, 0)
    din[p] = dout[p]

    near_sum(ORDER[3])

    wait(g_z.at[pl.ds(0, 31)], gz_r)
    g_xy[p] = jnp.sum(g_z[...], axis=0)

    def g_spread(o, carry):
        xx, yy = lax.rem(x + lax.div(o, 4), 4), lax.rem(y + lax.rem(o, 4), 4)
        send(g_xy.at[p], g_xy.at[p], gx_s, gx_r, plane(xx, yy))
        return carry

    lax.fori_loop(1, 16, g_spread, 0)

    wait(din.at[pl.ds(0, 15)], a_r)
    gain_all = gain_ref[...].astype(F32)
    for b in range(3):
        part = pl.ds(16 * b, 16)
        d = jnp.concatenate([din[q, part] for q in range(16)], axis=1).astype(F32)
        scaled = gain_all * d
        hat = xhat[part]
        stat = jnp.mean(scaled * hat, axis=-1, keepdims=True)
        dt_ref[part] = (root[part, 0:1] * (scaled - hat * stat)).astype(BF16)

    total = s_own[...]
    for k in range(3):
        wait(sr.at[k], q_r.at[k])
        total = total + sr[k].astype(F32)
    wg_ref[...] = total

    wait(g_xy.at[pl.ds(0, 15)], gx_r)
    gg_ref[...] = g_xy[...]

    for t in range(3):
        for r in range(2):
            wait(one(0, r, 0), za_s.at[t, r])
        wait(ss.at[t], q_s.at[t])
    for s in range(15):
        wait(wbuf.at[0], w_s.at[s])
    wait(xs.at[pl.ds(0, 15)], x_s)
    wait(xall.at[pl.ds(0, 16), 0], xb_s)
    for rel in range(4):
        for r in range(2):
            for k in range(6):
                wait(one(rel, r, 0) if k < 3 else line(rel, r, 0), c_s.at[rel, r, k])
        wait(gr.at[rel], g_s.at[rel])
        wait(dsend.at[pl.ds(0, 4)], e_s.at[rel])
    wait(dout.at[pl.ds(0, 15)], a_s)
    wait(g_z.at[pl.ds(0, 31)], gz_s)
    wait(g_xy.at[pl.ds(0, 15)], gx_s)


def local(tokens, norm_gain, kv_cotangent, weight_codes, block_scales):
    vmem, dma = pltpu.VMEM, pltpu.SemaphoreType.DMA
    hbm_spec, vmem_spec = pl.BlockSpec(memory_space=pltpu.HBM), pl.BlockSpec(memory_space=pltpu.VMEM)
    d_tokens, gain_grad, grads = pl.pallas_call(
        kernel,
        out_shape=(
            jax.ShapeDtypeStruct((48, 4096), BF16),
            jax.ShapeDtypeStruct((16, 1, 256), F32),
            jax.ShapeDtypeStruct((64, 256), F32),
        ),
        in_specs=[hbm_spec, vmem_spec, hbm_spec, hbm_spec, hbm_spec],
        out_specs=[vmem_spec] * 3,
        scratch_shapes=[
            vmem((1, 64, 256), BF16),
            vmem((1, 64), BF16),
            vmem((4, 4, 4, 96, 256), BF16),
            vmem((16, 64, 256), BF16),
            vmem((48, 4096), BF16),
            vmem((48, 4096), F32),
            vmem((48, 128), F32),
            vmem((16, 48, 256), BF16),
            vmem((16, 2, 48, 256), BF16),
            vmem((1536, 256), BF16),
            vmem((256, 1536), BF16),
            vmem((16, 2, 48, 256), F32),
            vmem((16, 48, 256), BF16),
            vmem((16, 48, 256), BF16),
            vmem((16, 48, 256), BF16),
            vmem((16, 48, 256), BF16),
            vmem((4, 4, 64, 256), BF16),
            vmem((4, 3, 64, 256), BF16),
            vmem((64, 256), F32),
            vmem((3, 64, 256), BF16),
            vmem((3, 64, 256), BF16),
            vmem((32, 1, 256), F32),
            vmem((16, 1, 256), F32),
            dma, dma, dma, dma,
            dma((3, 2)), dma((3, 2)),
            dma((15,)), dma((15,)),
            dma, dma, dma, dma,
            dma((4, 2, 6)), dma((4, 2, 6)),
            dma((4,)), dma((4,)),
            dma((3,)), dma((3,)),
            dma((4,)), dma((4,)),
            dma, dma, dma, dma, dma, dma,
        ],
        compiler_params=pltpu.CompilerParams(
            collective_id=0, has_side_effects=True, vmem_limit_bytes=52 * 1024 * 1024
        ),
    )(tokens, norm_gain.reshape(1, 4096), kv_cotangent, weight_codes, block_scales)
    return d_tokens, gain_grad.reshape(4096), grads.reshape(1, 64, 256)


def solution(mesh):
    placed = (P("fsdp", None), P(), P("fsdp", "node"), P("node", "fsdp", None), P("node", "fsdp"))
    return jax.shard_map(
        local,
        mesh=mesh,
        in_specs=placed,
        out_specs=(P(("fsdp", "node"), None), P(), P("node", "fsdp", None)),
        check_vma=False,
    )
```

time: 84.2 us -> 74.1 us (0.88)
  Pallas kernels: 76.1 us -> 68.2 us
  local copies, waits for them, and re-layouts: 6.92 us -> 5.03 us
    pallas_call x1, Pallas kernels: 76.1 us -> 68.2 us  [local(): pl.pallas_call(kernel, out_shape=(jax.ShapeDtypeStruct((48, 4096), BF16),...]
    unnamed x11 -> x9, local copies, waits for them, and re-layouts: 6.21 us -> 4.32 us
where the time goes in v2:
time: 74.1 us; the launch traced here: 73.8 us
  Pallas kernels  68.2 us (92%)
  local copies, waits for them, and re-layouts  5.03 us (7%)
    pallas_call x1, Pallas kernels, local(): pl.pallas_call(kernel, out_shape=(jax.ShapeDtypeStruct((48, 4096), BF16),...  68.2 us
    unnamed x9, local copies, waits for them, and re-layouts  4.32 us

profile of v2, /device:TPU:1, one launch (start us, length us, event | category | flops | bytes accessed | tf_op | source)
XLA Modules:
  0.0 73.8 jit_solution(17874976039866769839)
XLA Ops:
  0.6 0.7 reshape.15.gain_ref
  1.3 0.0 copy-start
  1.4 0.9 %copy-done = bf16[384,256]{1,0:T(8,128)(2,1)S(1)} copy-done((bf16[384,256]{1,0:T(8,128)(2,1)S(1)}, bf16[384,256]{1,0:T(8,128)(2,1)}, u32[]{:S(2)}) %copy-start) | copy-done | bytes 196632
  2.3 0.0 copy-start.1
  2.3 0.8 %copy-done.1 = bf16[1,64,256]{2,1,0:T(8,128)(2,1)S(1)} copy-done((bf16[1,64,256]{2,1,0:T(8,128)(2,1)S(1)}, bf16[1,64,256]{2,1,0:T(8,128)(2,1)}, u32[]{:S(2)}) %copy-start.1) | copy-done | bytes 32792
  3.0 0.0 copy-start.2
  3.0 0.7 copy-done.2
  3.7 68.2 %shard_map.76 = (bf16[48,4096]{1,0:T(8,128)(2,1)S(1)}, f32[16,1,256]{2,1,0:T(1,128)S(1)}, f32[64,256]{1,0:T(8,128)S(1)}) custom-call(bf16[384,4096]{1,0:T(8,128)(2,1)} %tok_hbm.1, bf16[1,4096]{1,0:T(2,128)(2,1)S(1)} %reshape.15.gain_ref, bf16[384,256]{1,0:T(8,128)(2,1)S(1)} %copy-done, bf16[1,64,256]{2,1,0:T(8,128)(2,1)S(1)} %copy-done.1, ...), custom_call_target="tpu_custom_call" | custom-call | tf_op jit(solution)/shard_map/pallas_call | solution.py:351
  71.9 0.7 %copy.11 = bf16[48,4096]{1,0:T(8,128)(2,1)} copy(bf16[48,4096]{1,0:T(8,128)(2,1)S(1)} %get-tuple-element.12) | data formatting | bytes 786432
  72.6 0.6 copy.12
  73.2 0.6 copy.13
Async XLA Ops:
  1.3 0.9 %copy-start = (bf16[384,256]{1,0:T(8,128)(2,1)S(1)}, bf16[384,256]{1,0:T(8,128)(2,1)}, u32[]{:S(2)}) copy-start(bf16[384,256]{1,0:T(8,128)(2,1)} %kv_hbm.1) | copy-start | bytes 589828
  2.3 0.8 %copy-start.1 = (bf16[1,64,256]{2,1,0:T(8,128)(2,1)S(1)}, bf16[1,64,256]{2,1,0:T(8,128)(2,1)}, u32[]{:S(2)}) copy-start(bf16[1,64,256]{2,1,0:T(8,128)(2,1)} %codes_hbm.1) | copy-start | bytes 98308
  3.0 0.7 copy-start.2

commit v3 on v2

--- a/solution.py
+++ b/solution.py
@@ -13,13 +13,13 @@
 
 
 def kernel(
-    tok_hbm, gain_ref, kv_hbm, codes_hbm, scales_hbm,
+    tok_hbm, gain_hbm, kv_hbm, codes_hbm, scales_hbm,
     dt_ref, gg_ref, wg_ref,
-    codes_ref, scales_ref, cot, wbuf, tok_v, xhat, root, xs, xall, xn, xt,
+    gain_ref, gain_row, codes_ref, scales_ref, cot, wbuf, tok_v, xhat, root, xs, xall, xn, xt,
     dn, dsend, drecv, dout, din,
     gs, gr, s_own, ss, sr,
     g_z, g_xy,
-    code_sem, scale_sem, tok_sem, own_sem, za_s, za_r, w_s, w_r, x_s, x_r, xb_s, xb_r,
+    gain_sem, code_sem, scale_sem, tok_sem, own_sem, za_s, za_r, w_s, w_r, x_s, x_r, xb_s, xb_r,
     c_s, c_r, g_s, g_r, q_s, q_r, e_s, e_r, a_s, a_r,
     gz_s, gz_r, gx_s, gx_r,
 ):
@@ -51,7 +51,9 @@
     )
     code_copy = pltpu.make_async_copy(codes_hbm, codes_ref, code_sem)
     scale_copy = pltpu.make_async_copy(scales_hbm, scales_ref, scale_sem)
+    gain_copy = pltpu.make_async_copy(gain_hbm, gain_ref, gain_sem)
     code_copy.start()
+    gain_copy.start()
     scale_copy.start()
     tok_copy.start()
     own_copy = pltpu.make_async_copy(
@@ -96,6 +98,9 @@
         for q in range(16):
             xs[q, part] = hat[:, 256 * q : 256 * (q + 1)].astype(BF16)
     xall[p, c] = xs[p]
+
+    gain_copy.wait()
+    gain_row[...] = gain_ref[...].astype(F32).reshape(1, 4096)
 
     pl.semaphore_wait(barrier, 46)
 
@@ -207,41 +212,40 @@
         block = cot[rel, xi].reshape(384, 256)
         return lax.dot_general(block, head, (((1,), (1,)), ((), ())), preferred_element_type=F32)
 
-    gain_here = gain_ref[:, pl.ds(pl.multiple_of(p * 256, 256), 256)].astype(F32)
-
+    gain_here = gain_row[:, pl.ds(pl.multiple_of(p * 256, 256), 256)]
+
+    w_round(0)
     share(1)
     share(3)
     stage(0, 0)
+    share(2)
     lax.fori_loop(1, 16, x_push, 0)
     stage(0, 1)
-    w_round(0)
-    share(2)
+    w_round(1)
     stage(1, 0)
     stage(2, 0)
     stage(0, 2)
-    wait(xall.at[pl.ds(0, 15), 0], x_r)
-    send(xall.at[pl.ds(0, 16), c], xall.at[pl.ds(0, 16), c], xb_s, xb_r, sibling)
-    w_round(1)
+    w_round(2)
     stage(1, 1)
     stage(2, 1)
     stage(3, 0)
     stage(0, 3)
+    wait(xall.at[pl.ds(0, 15), 0], x_r)
+    send(xall.at[pl.ds(0, 16), c], xall.at[pl.ds(0, 16), c], xb_s, xb_r, sibling)
+    w_round(3)
+    stage(1, 2)
+    stage(2, 2)
+    stage(3, 1)
     wait(xall.at[pl.ds(0, 16), 1 - c], xb_r)
     for q in range(16):
         xn[pl.ds(96 * q, 96)] = (xall[q].reshape(96, 256).astype(F32) * gain_here).astype(BF16)
     for q in range(12):
         xt[:, 128 * q : 128 * (q + 1)] = xn[128 * q : 128 * (q + 1)].T
-    w_round(2)
-    stage(1, 2)
-    stage(2, 2)
     grads(ORDER[0])
-    stage(3, 1)
-    w_round(3)
     stage(1, 3)
     grads(ORDER[1])
     stage(2, 3)
     grads(ORDER[2])
-    near_sum(ORDER[0])
     w_round(4)
 
     def three(xi, carry):
@@ -250,8 +254,6 @@
         return carry
 
     lax.fori_loop(0, 4, three, 0)
-    near_sum(ORDER[1])
-    near_sum(ORDER[2])
     stage(3, 2)
     stage(3, 3)
 
@@ -295,6 +297,9 @@
     lax.fori_loop(0, 4, turn, 0)
     din[p] = dout[p]
 
+    near_sum(ORDER[1])
+    near_sum(ORDER[2])
+    near_sum(ORDER[0])
     near_sum(ORDER[3])
 
     wait(g_z.at[pl.ds(0, 31)], gz_r)
@@ -308,7 +313,7 @@
     lax.fori_loop(1, 16, g_spread, 0)
 
     wait(din.at[pl.ds(0, 15)], a_r)
-    gain_all = gain_ref[...].astype(F32)
+    gain_all = gain_row[...]
     for b in range(3):
         part = pl.ds(16 * b, 16)
         d = jnp.concatenate([din[q, part] for q in range(16)], axis=1).astype(F32)
@@ -355,9 +360,11 @@
             jax.ShapeDtypeStruct((16, 1, 256), F32),
             jax.ShapeDtypeStruct((64, 256), F32),
         ),
-        in_specs=[hbm_spec, vmem_spec, hbm_spec, hbm_spec, hbm_spec],
+        in_specs=[hbm_spec] * 5,
         out_specs=[vmem_spec] * 3,
         scratch_shapes=[
+            vmem((4096,), BF16),
+            vmem((1, 4096), F32),
             vmem((1, 64, 256), BF16),
             vmem((1, 64), BF16),
             vmem((4, 4, 4, 96, 256), BF16),
@@ -381,7 +388,7 @@
             vmem((3, 64, 256), BF16),
             vmem((32, 1, 256), F32),
             vmem((16, 1, 256), F32),
-            dma, dma, dma, dma,
+            dma, dma, dma, dma, dma,
             dma((3, 2)), dma((3, 2)),
             dma((15,)), dma((15,)),
             dma, dma, dma, dma,
@@ -394,7 +401,7 @@
         compiler_params=pltpu.CompilerParams(
             collective_id=0, has_side_effects=True, vmem_limit_bytes=52 * 1024 * 1024
         ),
-    )(tokens, norm_gain.reshape(1, 4096), kv_cotangent, weight_codes, block_scales)
+    )(*[pltpu.with_memory_space_constraint(a, pltpu.HBM) for a in (tokens, norm_gain, kv_cotangent, weight_codes, block_scales)])
     return d_tokens, gain_grad.reshape(4096), grads.reshape(1, 64, 256)
 
 

time: 74.1 us -> 67.8 us (0.915)
  Pallas kernels: 68.2 us -> 65.1 us
  local copies, waits for them, and re-layouts: 5.03 us -> 1.98 us
    pallas_call x1, Pallas kernels: 68.2 us -> 65.1 us  [local(): pl.pallas_call(kernel, out_shape=(jax.ShapeDtypeStruct((48, 4096), BF16),...]
    unnamed x9 -> x3, local copies, waits for them, and re-layouts: 4.32 us -> 1.98 us
where the time goes in v3:
time: 67.8 us; the launch traced here: 67.7 us
  Pallas kernels  65.1 us (96%)
  local copies, waits for them, and re-layouts  1.98 us (3%)
    pallas_call x1, Pallas kernels, local(): pl.pallas_call(kernel, out_shape=(jax.ShapeDtypeStruct((48, 4096), BF16),...  65.1 us
    unnamed x3, local copies, waits for them, and re-layouts  1.98 us

profile of v3, /device:TPU:1, one launch (start us, length us, event | category | flops | bytes accessed | tf_op | source)
XLA Modules:
  0.0 67.7 jit_solution(829951718494194984)
XLA Ops:
  0.6 65.1 %shard_map.76 = (bf16[48,4096]{1,0:T(8,128)(2,1)S(1)}, f32[16,1,256]{2,1,0:T(1,128)S(1)}, f32[64,256]{1,0:T(8,128)S(1)}) custom-call(bf16[384,4096]{1,0:T(8,128)(2,1)} %tok_hbm.1, bf16[4096]{0:T(1024)(128)(2,1)} %gain_hbm.1, bf16[384,256]{1,0:T(8,128)(2,1)} %kv_hbm.1, bf16[1,64,256]{2,1,0:T(8,128)(2,1)} %codes_hbm.1, bf16[1,64]{1,0:T(2,128)(2,1)} %scales_hbm.1), custom_call_target="tpu_custom_call" | custom-call | tf_op jit(solution)/shard_map/pallas_call | solution.py:356
  65.7 0.7 %copy.11 = bf16[48,4096]{1,0:T(8,128)(2,1)} copy(bf16[48,4096]{1,0:T(8,128)(2,1)S(1)} %get-tuple-element.12) | data formatting | bytes 786432
  66.4 0.6 copy.12
  67.1 0.6 copy.13

commit v4 on v3

--- a/solution.py
+++ b/solution.py
@@ -219,8 +219,8 @@
     share(3)
     stage(0, 0)
     share(2)
+    stage(0, 1)
     lax.fori_loop(1, 16, x_push, 0)
-    stage(0, 1)
     w_round(1)
     stage(1, 0)
     stage(2, 0)
@@ -258,7 +258,7 @@
     stage(3, 3)
 
     def last(j, gain_sum):
-        xi = lax.rem(x + j, 4)
+        xi = lax.rem(x + j + 2, 4)
         mine = pl.ds(4 * xi, 4)
         total = dn[mine] + times_w(ORDER[3], xi).reshape(4, 2, 48, 256)
         dn[mine] = total
@@ -278,15 +278,15 @@
     grads(ORDER[3])
 
     def turn(j, carry):
-        xi = lax.rem(x + j, 4)
+        xi = lax.rem(x + j + 2, 4)
         mine = pl.ds(4 * xi, 4)
         wait(drecv.at[mine], e_r.at[j])
         dout[mine] = (dn[mine, c] + drecv[mine].astype(F32)).astype(BF16)
 
         def spread(o, inner):
-            yy = lax.rem(y + o, 4)
-
-            @pl.when(j * 4 + o > 0)
+            yy = lax.rem(y + o + 2, 4)
+
+            @pl.when(lax.rem(j + 2, 4) * 4 + lax.rem(o + 2, 4) > 0)
             def _():
                 send(dout.at[xi * 4 + yy], din.at[p], a_s, a_r, plane(xi, yy))
 
@@ -299,8 +299,8 @@
 
     near_sum(ORDER[1])
     near_sum(ORDER[2])
+    near_sum(ORDER[3])
     near_sum(ORDER[0])
-    near_sum(ORDER[3])
 
     wait(g_z.at[pl.ds(0, 31)], gz_r)
     g_xy[p] = jnp.sum(g_z[...], axis=0)
@@ -312,29 +312,9 @@
 
     lax.fori_loop(1, 16, g_spread, 0)
 
-    wait(din.at[pl.ds(0, 15)], a_r)
-    gain_all = gain_row[...]
-    for b in range(3):
-        part = pl.ds(16 * b, 16)
-        d = jnp.concatenate([din[q, part] for q in range(16)], axis=1).astype(F32)
-        scaled = gain_all * d
-        hat = xhat[part]
-        stat = jnp.mean(scaled * hat, axis=-1, keepdims=True)
-        dt_ref[part] = (root[part, 0:1] * (scaled - hat * stat)).astype(BF16)
-
-    total = s_own[...]
-    for k in range(3):
-        wait(sr.at[k], q_r.at[k])
-        total = total + sr[k].astype(F32)
-    wg_ref[...] = total
-
-    wait(g_xy.at[pl.ds(0, 15)], gx_r)
-    gg_ref[...] = g_xy[...]
-
     for t in range(3):
         for r in range(2):
             wait(one(0, r, 0), za_s.at[t, r])
-        wait(ss.at[t], q_s.at[t])
     for s in range(15):
         wait(wbuf.at[0], w_s.at[s])
     wait(xs.at[pl.ds(0, 15)], x_s)
@@ -345,6 +325,28 @@
                 wait(one(rel, r, 0) if k < 3 else line(rel, r, 0), c_s.at[rel, r, k])
         wait(gr.at[rel], g_s.at[rel])
         wait(dsend.at[pl.ds(0, 4)], e_s.at[rel])
+
+    wait(din.at[pl.ds(0, 15)], a_r)
+    gain_all = gain_row[...]
+    for b in range(3):
+        part = pl.ds(16 * b, 16)
+        d = jnp.concatenate([din[q, part] for q in range(16)], axis=1).astype(F32)
+        scaled = gain_all * d
+        hat = xhat[part]
+        stat = jnp.mean(scaled * hat, axis=-1, keepdims=True)
+        dt_ref[part] = (root[part, 0:1] * (scaled - hat * stat)).astype(BF16)
+
+    total = s_own[...]
+    for k in range(3):
+        wait(sr.at[k], q_r.at[k])
+        total = total + sr[k].astype(F32)
+    wg_ref[...] = total
+
+    wait(g_xy.at[pl.ds(0, 15)], gx_r)
+    gg_ref[...] = g_xy[...]
+
+    for t in range(3):
+        wait(ss.at[t], q_s.at[t])
     wait(dout.at[pl.ds(0, 15)], a_s)
     wait(g_z.at[pl.ds(0, 31)], gz_s)
     wait(g_xy.at[pl.ds(0, 15)], gx_s)

time: 67.8 us -> 67.5 us (level)
  no operation moved by 1% of the time
where the time goes in v4:
time: 67.5 us; the launch traced here: 67.3 us
  Pallas kernels  64.7 us (96%)
  local copies, waits for them, and re-layouts  1.98 us (3%)
    pallas_call x1, Pallas kernels, local(): pl.pallas_call(kernel, out_shape=(jax.ShapeDtypeStruct((48, 4096), BF16),...  64.7 us
    unnamed x3, local copies, waits for them, and re-layouts  1.98 us

profile of v4, /device:TPU:1, one launch (start us, length us, event | category | flops | bytes accessed | tf_op | source)
XLA Modules:
  0.0 67.3 jit_solution(5592111651722646095)
XLA Ops:
  0.6 64.7 %shard_map.76 = (bf16[48,4096]{1,0:T(8,128)(2,1)S(1)}, f32[16,1,256]{2,1,0:T(1,128)S(1)}, f32[64,256]{1,0:T(8,128)S(1)}) custom-call(bf16[384,4096]{1,0:T(8,128)(2,1)} %tok_hbm.1, bf16[4096]{0:T(1024)(128)(2,1)} %gain_hbm.1, bf16[384,256]{1,0:T(8,128)(2,1)} %kv_hbm.1, bf16[1,64,256]{2,1,0:T(8,128)(2,1)} %codes_hbm.1, bf16[1,64]{1,0:T(2,128)(2,1)} %scales_hbm.1), custom_call_target="tpu_custom_call" | custom-call | tf_op jit(solution)/shard_map/pallas_call | solution.py:358
  65.3 0.7 %copy.11 = bf16[48,4096]{1,0:T(8,128)(2,1)} copy(bf16[48,4096]{1,0:T(8,128)(2,1)S(1)} %get-tuple-element.12) | data formatting | bytes 786432
  66.1 0.6 copy.12
  66.7 0.6 copy.13

commit v5 on v3

--- a/solution.py
+++ b/solution.py
@@ -299,7 +299,6 @@
 
     near_sum(ORDER[1])
     near_sum(ORDER[2])
-    near_sum(ORDER[0])
     near_sum(ORDER[3])
 
     wait(g_z.at[pl.ds(0, 31)], gz_r)
@@ -311,6 +310,7 @@
         return carry
 
     lax.fori_loop(1, 16, g_spread, 0)
+    near_sum(ORDER[0])
 
     wait(din.at[pl.ds(0, 15)], a_r)
     gain_all = gain_row[...]

time: 67.8 us -> 67.8 us (level)
  no operation moved by 1% of the time
where the time goes in v5:
time: 67.8 us; the launch traced here: 67.7 us
  Pallas kernels  65.1 us (96%)
  local copies, waits for them, and re-layouts  1.98 us (3%)
    pallas_call x1, Pallas kernels, local(): pl.pallas_call(kernel, out_shape=(jax.ShapeDtypeStruct((48, 4096), BF16),...  65.1 us
    unnamed x3, local copies, waits for them, and re-layouts  1.98 us

profile of v5, /device:TPU:1, one launch (start us, length us, event | category | flops | bytes accessed | tf_op | source)
XLA Modules:
  0.0 67.7 jit_solution(17342079331882272503)
XLA Ops:
  0.6 65.1 %shard_map.76 = (bf16[48,4096]{1,0:T(8,128)(2,1)S(1)}, f32[16,1,256]{2,1,0:T(1,128)S(1)}, f32[64,256]{1,0:T(8,128)S(1)}) custom-call(bf16[384,4096]{1,0:T(8,128)(2,1)} %tok_hbm.1, bf16[4096]{0:T(1024)(128)(2,1)} %gain_hbm.1, bf16[384,256]{1,0:T(8,128)(2,1)} %kv_hbm.1, bf16[1,64,256]{2,1,0:T(8,128)(2,1)} %codes_hbm.1, bf16[1,64]{1,0:T(2,128)(2,1)} %scales_hbm.1), custom_call_target="tpu_custom_call" | custom-call | tf_op jit(solution)/shard_map/pallas_call | solution.py:356
  65.7 0.7 %copy.11 = bf16[48,4096]{1,0:T(8,128)(2,1)} copy(bf16[48,4096]{1,0:T(8,128)(2,1)S(1)} %get-tuple-element.12) | data formatting | bytes 786432
  66.4 0.6 copy.12
  67.1 0.6 copy.13
